TPU v7x, 256 devices: a whole 4x4x8 slice. The times are simulated.
256 devices in a mesh: blk: 32 (over y, z), head: 2 (over core), clip: 4 (over x).
Axes of the slice: x: 4, y: 4, z: 8, core: 2. Of those that a mesh axis runs over, the one named last changes fastest.
Arguments:
- tokens: bfloat16 [36864, 1536], P(('clip', 'blk', 'head')), parts along dimension 0, may hold values from -6 to 6
- modulation: float32 [12, 1536], P('clip'), parts along dimension 0, may hold values from -3 to 3
- w_qkv: bfloat16 [1536, 3, 1536], P(None, None, 'head'), may hold values from -0.25 to 0.25
- w_out: bfloat16 [1536, 1536], P('head'), may hold values from -0.15625 to 0.15625
- w_cross: bfloat16 [1536, 1536], P(None, 'head'), may hold values from -0.15625 to 0.15625
- q_gain: float32 [128], replicated, may hold values from 0.5 to 6
- k_gain: float32 [128], replicated, may hold values from 0.5 to 6
- cross_gain: float32 [128], replicated, may hold values from 0.5 to 6
- scene_keys: bfloat16 [8192, 1536], P(('clip', 'blk'), 'head'), parts along dimension 0, may hold values from -40 to 40
- scene_values: bfloat16 [8192, 1536], P(('clip', 'blk'), 'head'), parts along dimension 0, may hold values from -6 to 6
Outputs:
- hidden: bfloat16 [36864, 1536], P(('clip', 'blk', 'head')), parts along dimension 0
- cross_context: bfloat16 [36864, 1536], P(('clip', 'blk'), 'head'), parts along dimension 0
There are 4 independent parts, one for each index of `clip`. A program takes and returns all parts, laid end to end along the dimension named above; an argument that names none is the same for every part. Nothing has to cross between parts.
All inputs are finite; a program needn't handle non-finite values.
Results may differ from a plain program's by a relative error of at most 0.015.
The roundings to bfloat16 on the way count: a program that leaves them out, or rounds other values in their place, can miss the bound.
Values may be sent and summed in bfloat16 or wider, within the bound.
A program may use at most 128 MiB of HBM per device.

v0:
```python
import jax
import jax.numpy as jnp
from jax import lax
from jax.sharding import PartitionSpec as P

HD = 128


def head_norm(values, gain):
    rms = jnp.mean(values * values, axis=-1, keepdims=True)
    return values * lax.rsqrt(rms + 1e-06) * gain


def attend_block(carry, queries, keys_blk, values_blk):
    best, total, accum = carry
    count = keys_blk.shape[0]
    heads_here = queries.shape[1]
    width = queries.shape[2]
    keys_three = keys_blk.reshape(count, heads_here, width)
    values_three = values_blk.reshape(count, heads_here, width).astype(jnp.float32)
    scores = jnp.einsum("rhd,nhd->hrn", queries, keys_three, preferred_element_type=jnp.float32) * (
        1.0 / width**0.5
    )
    newbest = jnp.maximum(best, jnp.max(scores, axis=-1))
    factor = jnp.exp(best - newbest)
    weights = jnp.exp(scores - newbest[..., None])
    total = total * factor + jnp.sum(weights, axis=-1)
    accum = accum * jnp.transpose(factor)[..., None] + jnp.einsum(
        "hrn,nhd->rhd", weights, values_three
    )
    return (newbest, total, accum)


def attend_keys(carry, queries, keys_rows, values_rows):
    count = keys_rows.shape[0]
    blocks = count // 1024
    keys_split = keys_rows.reshape(blocks, 1024, keys_rows.shape[1])
    values_split = values_rows.reshape(blocks, 1024, values_rows.shape[1])

    def advance(state, pair):
        return (attend_block(state, queries, pair[0], pair[1]), None)

    carry, unused = lax.scan(advance, carry, (keys_split, values_split))
    return carry


def start_state(queries):
    rows = queries.shape[0]
    heads_here = queries.shape[1]
    best = jnp.full((heads_here, rows), -1e30, jnp.float32)
    total = jnp.zeros((heads_here, rows), jnp.float32)
    accum = jnp.zeros(queries.shape, jnp.float32)
    return (best, total, accum)


def finish_state(state):
    best, total, accum = state
    result = accum / jnp.transpose(total)[..., None]
    return result.reshape(result.shape[0], result.shape[1] * result.shape[2]).astype(jnp.bfloat16)


def shards(
    tokens, modulation, w_qkv, w_out, w_cross, q_gain, k_gain, cross_gain, scene_keys, scene_values
):
    width = tokens.shape[1]
    local_width = w_qkv.shape[2]
    heads_here = local_width // HD
    rows_raw = lax.all_gather(tokens, "head", axis=0, tiled=True)
    rows_count = rows_raw.shape[0]
    xfloat = rows_raw.astype(jnp.float32)
    mean = jnp.mean(xfloat, axis=-1, keepdims=True)
    var = jnp.mean((xfloat - mean) ** 2, axis=-1, keepdims=True)
    normed = (xfloat - mean) * lax.rsqrt(var + 1e-06)
    modulated = (normed * (1.0 + modulation[1]) + modulation[0]).astype(jnp.bfloat16)
    projected = jnp.dot(
        modulated, w_qkv.reshape(width, 3 * local_width), preferred_element_type=jnp.float32
    )
    projected = projected.reshape(rows_count, 3, heads_here, HD)
    queries = head_norm(projected[:, 0], q_gain).astype(jnp.bfloat16)
    keys_flat = (
        head_norm(projected[:, 1], k_gain).astype(jnp.bfloat16).reshape(rows_count, local_width)
    )
    values_flat = projected[:, 2].astype(jnp.bfloat16).reshape(rows_count, local_width)
    pieces = (
        lax.all_gather(keys_flat, "blk", axis=0, tiled=True),
        lax.all_gather(values_flat, "blk", axis=0, tiled=True),
    )
    state = attend_keys(start_state(queries), queries, pieces[0], pieces[1])
    context = finish_state(state)
    partial_sum = jnp.dot(context, w_out, preferred_element_type=jnp.float32)
    mine = lax.psum_scatter(partial_sum, "head", scatter_dimension=0, tiled=True)
    hidden = (tokens.astype(jnp.float32) + modulation[2] * mine).astype(jnp.bfloat16)
    hidden_all = lax.all_gather(hidden, "head", axis=0, tiled=True)
    cross_proj = jnp.dot(hidden_all, w_cross, preferred_element_type=jnp.float32).reshape(
        rows_count, heads_here, HD
    )
    cross_queries = head_norm(cross_proj, cross_gain).astype(jnp.bfloat16)
    pieces = (
        lax.all_gather(scene_keys, "blk", axis=0, tiled=True),
        lax.all_gather(scene_values, "blk", axis=0, tiled=True),
    )
    scene_state = attend_keys(start_state(cross_queries), cross_queries, pieces[0], pieces[1])
    cross_context = finish_state(scene_state)
    return (hidden, cross_context)


def solution(mesh):
    return jax.shard_map(
        shards,
        mesh=mesh,
        in_specs=(
            P(("clip", "blk", "head"), None),
            P("clip", None),
            P(None, None, "head"),
            P("head", None),
            P(None, "head"),
            P(),
            P(),
            P(),
            P(("clip", "blk"), "head"),
            P(("clip", "blk"), "head"),
        ),
        out_specs=(P(("clip", "blk", "head"), None), P(("clip", "blk"), "head")),
        check_vma=False,
    )
```

profile of v0, /device:TPU:2, one launch (start us, length us, event | category | flops | bytes accessed | tf_op | source)
XLA Modules:
  0.0 703.8 jit_solution(5438818760283527297)
XLA Ops:
  10.7 10.3 %copy.64 = bf16[1536,3,768]{0,2,1:T(8,128)(2,1)} copy(bf16[1536,3,768]{2,0,1:T(8,128)(2,1)} %param.16) | data formatting | bytes 14155776 | tf_op args[2]
  21.0 5.0 fusion.37
  36.4 124.1 %all-gather.5.cloned.1.call-done = bf16[9216,768]{1,0:T(8,128)(2,1)} async-done(((bf16[288,768]{1,0:T(8,128)(2,1)}), bf16[9216,768]{1,0:T(8,128)(2,1)}) %all-gather.5.cloned.1.call-update) | async-done | bytes 14155792 | tf_op jit(solution)/shard_map/all_gather | solution.py:85
  160.4 126.9 %all-gather.7.cloned.1.call-done = bf16[9216,768]{1,0:T(8,128)(2,1)} async-done(((bf16[288,768]{1,0:T(8,128)(2,1)}), bf16[9216,768]{1,0:T(8,128)(2,1)}) %all-gather.7.cloned.1.call-update) | async-done | bytes 14155792 | tf_op jit(solution)/shard_map/all_gather | solution.py:86
  287.3 194.9 %while.30 = (s32[]{:T(128)}, f32[6,288]{1,0:T(8,128)S(1)}, f32[6,288]{1,0:T(8,128)S(1)}, f32[288,6,128]{2,0,1:T(8,128)S(1)}, bf16[9,1024,768]{2,1,0:T(8,128)(2,1...) while((s32[]{:T(128)}, f32[6,288]{1,0:T(8,128)S(1)}, ...), condition=%wide.region_7.8_spmd.clone, body=%wide.region_4.7_spmd.clone.sunk | while | flops 919029888 | bytes 67596424 | solution.py:43
  293.7 5.5 bitcast_reduce_fusion.4
  315.3 5.5 bitcast_reduce_fusion.4
  323.4 4.7 fusion.88
  337.0 5.5 bitcast_reduce_fusion.4
  345.1 4.7 fusion.88
  358.6 5.5 bitcast_reduce_fusion.4
  366.7 4.7 fusion.88
  380.3 5.5 bitcast_reduce_fusion.4
  402.0 5.5 bitcast_reduce_fusion.4
  410.0 4.7 fusion.88
  423.6 5.5 bitcast_reduce_fusion.4
  431.7 4.7 fusion.88
  445.3 5.5 bitcast_reduce_fusion.4
  453.4 4.7 fusion.88
  466.9 5.5 bitcast_reduce_fusion.4
  485.6 10.6 %reduce-scatter.2.cloned.1.call-done = f32[144,1536]{1,0:T(8,128)} async-done(((f32[288,1536]{1,0:T(8,128)}), f32[144,1536]{1,0:T(8,128)}) %reduce-scatter.2.cloned.1.call-update) | async-done | bytes 884752 | tf_op jit(solution)/shard_map/reduce_scatter | solution.py:91
  504.0 76.2 %all-gather.9.cloned.1.call-done = bf16[2048,768]{1,0:T(8,128)(2,1)} async-done(((bf16[64,768]{1,0:T(8,128)(2,1)}), bf16[2048,768]{1,0:T(8,128)(2,1)}) %all-gather.9.cloned.1.call-update) | async-done | bytes 3145744 | tf_op jit(solution)/shard_map/all_gather | solution.py:99
  580.2 79.4 %all-gather.11.cloned.1.call-done = bf16[2048,768]{1,0:T(8,128)(2,1)} async-done(((bf16[64,768]{1,0:T(8,128)(2,1)}), bf16[2048,768]{1,0:T(8,128)(2,1)}) %all-gather.11.cloned.1.call-update) | async-done | bytes 3145744 | tf_op jit(solution)/shard_map/all_gather | solution.py:100
  659.6 35.9 %while.31 = (s32[]{:T(128)}, f32[6,288]{1,0:T(8,128)S(1)}, f32[6,288]{1,0:T(8,128)S(1)}, f32[288,6,128]{2,0,1:T(8,128)S(1)}, bf16[2,1024,768]{2,1,0:T(8,128)(2,1...) while((s32[]{:T(128)}, f32[6,288]{1,0:T(8,128)S(1)}, ...), condition=%wide.region_13.14_spmd.clone, body=%wide.region_10.13_spmd.clone.sunk | while | flops 919029888 | bytes 67596424 | solution.py:43
  (169 shorter events, 179.3 us)
Async XLA Ops:
  7.2 475.1 %copy-start = (bf16[768,1536]{1,0:T(8,128)(2,1)S(1)}, bf16[768,1536]{1,0:T(8,128)(2,1)}, u32[]{:S(2)}) copy-start(bf16[768,1536]{1,0:T(8,128)(2,1)} %param.17) | copy-start | bytes 7077892
  7.2 3.5 copy-start.6
  7.2 153.3 %all-gather.5.cloned.1.call-start = ((), (), s32[]{:S(2)}) async-start(), calls=%async_computation.1 | async-start | bytes 14598144 | tf_op jit(solution)/shard_map/all_gather | solution.py:85
  26.0 1.6 copy-start.4
  27.6 1.1 copy-start.9
  30.1 4.0 copy-start.7
  30.1 257.2 %all-gather.7.cloned.1.call-start = ((), (), s32[]{:S(2)}) async-start(), calls=%async_computation.2 | async-start | bytes 14598144 | tf_op jit(solution)/shard_map/all_gather | solution.py:86
  32.5 463.7 %reduce-scatter.2.cloned.1.call-start = ((), (), s32[]{:S(2)}) async-start(), calls=%async_computation.3 | async-start | bytes 2654208 | tf_op jit(solution)/shard_map/reduce_scatter | solution.py:91
  301.8 5.5 copy-start.2
  323.4 5.5 copy-start.2
  345.1 5.5 copy-start.2
  366.7 5.5 copy-start.2
  388.4 5.5 copy-start.2
  410.0 5.5 copy-start.2
  431.7 5.5 copy-start.2
  453.4 5.5 copy-start.2
  475.0 5.5 copy-start.2
  484.4 95.8 %all-gather.9.cloned.1.call-start = ((), (), s32[]{:S(2)}) async-start(), calls=%async_computation.4 | async-start | bytes 3244032 | tf_op jit(solution)/shard_map/all_gather | solution.py:99
  485.0 174.6 %all-gather.11.cloned.1.call-start = ((), (), s32[]{:S(2)}) async-start(), calls=%async_computation.5 | async-start | bytes 3244032 | tf_op jit(solution)/shard_map/all_gather | solution.py:100
  497.6 2.6 copy-start.5
  502.8 0.8 copy-start.8
  670.8 5.1 copy-start.3
  688.7 5.1 copy-start.3
  695.5 1.8 copy-start.1
Sparse Core Ops, SparseCore 0:
  30.3 130.1 all-gather.4
  163.0 124.2 all-gather.6
  484.5 11.6 reduce-scatter.1
  499.0 81.1 all-gather.8
  583.0 76.5 all-gather.10
where the time goes:
time: 705 us; the launch traced here: 704 us
  waiting for transfers between devices  418 us (59%)
  local copies, waits for them, and re-layouts  120 us (17%)
  matrix products  118 us (17%)
  other arithmetic  27.2 us (4%)
  between operations  14.1 us (2%)
    all_gather x1, waiting for transfers between devices, shards(): lax.all_gather(values_flat, 'blk', axis=0, tiled=True)  127 us
    all_gather x1, waiting for transfers between devices, shards(): lax.all_gather(keys_flat, 'blk', axis=0, tiled=True)  124 us
    dynamic_slice x33, local copies, waits for them, and re-layouts, attend_keys(): carry, unused = lax.scan(advance, carry, (keys_split, values_split))  94.9 us
    all_gather x1, waiting for transfers between devices, shards(): lax.all_gather(scene_values, 'blk', axis=0, tiled=True)  79.4 us
    all_gather x1, waiting for transfers between devices, shards(): lax.all_gather(scene_keys, 'blk', axis=0, tiled=True)  76.2 us
    dot_general x11, matrix products, attend_block(): jnp.einsum('rhd,nhd->hrn', queries, keys_three, preferred_element_type=jn...  57.3 us
    dot_general x11, matrix products, attend_block(): jnp.einsum('hrn,nhd->rhd', weights, values_three)  51.1 us
    reduce_sum x11, other arithmetic, attend_block(): total = total * factor + jnp.sum(weights, axis=-1)  17.8 us
  transfers between devices with their start and end apart: 5, of which 5 were waited for; matrix products, arithmetic and copies ran while one was open for 2% of the time, Pallas kernels for 0%

commit v1 on v0

--- a/solution.py
+++ b/solution.py
@@ -97,7 +97,15 @@
     cross_queries = head_norm(cross_proj, cross_gain).astype(jnp.bfloat16)
     pieces = (
         lax.all_gather(scene_keys, "blk", axis=0, tiled=True),
-        lax.all_gather(scene_values, "blk", axis=0, tiled=True),
+        jnp.concatenate(
+            lax.all_to_all(
+                jnp.stack([scene_values for _ in range(lax.psum(1, axis_name="blk"))], 0),
+                split_axis=0,
+                concat_axis=0,
+                axis_name="blk",
+            ),
+            0,
+        ),
     )
     scene_state = attend_keys(start_state(cross_queries), cross_queries, pieces[0], pieces[1])
     cross_context = finish_state(scene_state)

time: 705 us -> 636 us (0.902)
  waiting for transfers between devices: 418 us -> 343 us
    all_gather x1 -> x0, waiting for transfers between devices: 79.4 us -> none  [shards(): lax.all_gather(scene_values, 'blk', axis=0, tiled=True)]
    all_to_all x0 -> x1, waiting for transfers between devices: none -> 70.4 us  [shards(): lax.all_to_all(jnp.stack([scene_values for _ in range(lax.psum(1, axis_na...]
    all_gather x1, waiting for transfers between devices: 76.2 us -> 17.4 us  [shards(): lax.all_gather(scene_keys, 'blk', axis=0, tiled=True)]
    reduce_scatter x1, waiting for transfers between devices: 10.6 us -> 3.33 us  [shards(): lax.psum_scatter(partial_sum, 'head', scatter_dimension=0, tiled=True)]
where the time goes in v1:
time: 636 us; the launch traced here: 634 us
  waiting for transfers between devices  343 us (54%)
  local copies, waits for them, and re-layouts  122 us (19%)
  matrix products  116 us (18%)
  other arithmetic  27.2 us (4%)
  between operations  14.1 us (2%)
    all_gather x1, waiting for transfers between devices, shards(): lax.all_gather(values_flat, 'blk', axis=0, tiled=True)  127 us
    all_gather x1, waiting for transfers between devices, shards(): lax.all_gather(keys_flat, 'blk', axis=0, tiled=True)  124 us
    dynamic_slice x33, local copies, waits for them, and re-layouts, attend_keys(): carry, unused = lax.scan(advance, carry, (keys_split, values_split))  94.9 us
    all_to_all x1, waiting for transfers between devices, shards(): lax.all_to_all(jnp.stack([scene_values for _ in range(lax.psum(1, axis_na...  70.4 us
    dot_general x11, matrix products, attend_block(): jnp.einsum('rhd,nhd->hrn', queries, keys_three, preferred_element_type=jn...  57.3 us
    dot_general x11, matrix products, attend_block(): jnp.einsum('hrn,nhd->rhd', weights, values_three)  51.1 us
    reduce_sum x11, other arithmetic, attend_block(): total = total * factor + jnp.sum(weights, axis=-1)  17.8 us
    all_gather x1, waiting for transfers between devices, shards(): lax.all_gather(scene_keys, 'blk', axis=0, tiled=True)  17.4 us
  transfers between devices with their start and end apart: 5, of which 5 were waited for; matrix products, arithmetic and copies ran while one was open for 2% of the time, Pallas kernels for 0%

profile of v1, /device:TPU:2, one launch (start us, length us, event | category | flops | bytes accessed | tf_op | source)
XLA Modules:
  0.0 634.4 jit_solution(8511148220994235086)
XLA Ops:
  10.7 10.3 %copy.64 = bf16[1536,3,768]{0,2,1:T(8,128)(2,1)} copy(bf16[1536,3,768]{2,0,1:T(8,128)(2,1)} %param.16) | data formatting | bytes 14155776 | tf_op args[2]
  21.0 5.0 fusion.37
  36.4 124.1 %all-gather.4.cloned.1.call-done = bf16[9216,768]{1,0:T(8,128)(2,1)} async-done(((bf16[288,768]{1,0:T(8,128)(2,1)}), bf16[9216,768]{1,0:T(8,128)(2,1)}) %all-gather.4.cloned.1.call-update) | async-done | bytes 14155792 | tf_op jit(solution)/shard_map/all_gather | solution.py:85
  160.4 126.9 %all-gather.6.cloned.1.call-done = bf16[9216,768]{1,0:T(8,128)(2,1)} async-done(((bf16[288,768]{1,0:T(8,128)(2,1)}), bf16[9216,768]{1,0:T(8,128)(2,1)}) %all-gather.6.cloned.1.call-update) | async-done | bytes 14155792 | tf_op jit(solution)/shard_map/all_gather | solution.py:86
  287.3 194.9 %while.30 = (s32[]{:T(128)}, f32[6,288]{1,0:T(8,128)S(1)}, f32[6,288]{1,0:T(8,128)S(1)}, f32[288,6,128]{2,0,1:T(8,128)S(1)}, bf16[9,1024,768]{2,1,0:T(8,128)(2,1...) while((s32[]{:T(128)}, f32[6,288]{1,0:T(8,128)S(1)}, ...), condition=%wide.region_7.8_spmd.clone, body=%wide.region_4.7_spmd.clone.sunk | while | flops 919029888 | bytes 67596424 | solution.py:43
  293.7 5.5 bitcast_reduce_fusion.4
  315.3 5.5 bitcast_reduce_fusion.4
  323.4 4.7 fusion.88
  337.0 5.5 bitcast_reduce_fusion.4
  345.1 4.7 fusion.88
  358.6 5.5 bitcast_reduce_fusion.4
  366.7 4.7 fusion.88
  380.3 5.5 bitcast_reduce_fusion.4
  402.0 5.5 bitcast_reduce_fusion.4
  410.0 4.7 fusion.88
  423.6 5.5 bitcast_reduce_fusion.4
  431.7 4.7 fusion.88
  445.3 5.5 bitcast_reduce_fusion.4
  453.4 4.7 fusion.88
  466.9 5.5 bitcast_reduce_fusion.4
  486.4 5.9 all-to-all-start
  502.4 70.4 %all-to-all-done = bf16[32,64,768]{2,1,0:T(8,128)(2,1)} async-done(((bf16[32,64,768]{2,1,0:T(8,128)(2,1)}), bf16[32,64,768]{2,1,0:T(8,128)(2,1)}, u32[]{:S(2)}, u32[]{:S(2)}) %all-to-all-start) | async-done | bytes 3145760 | tf_op jit(solution)/shard_map/all_to_all | solution.py:101
  572.8 17.4 %all-gather.8.cloned.1.call-done = bf16[2048,768]{1,0:T(8,128)(2,1)} async-done(((bf16[64,768]{1,0:T(8,128)(2,1)}), bf16[2048,768]{1,0:T(8,128)(2,1)}) %all-gather.8.cloned.1.call-update) | async-done | bytes 3145744 | tf_op jit(solution)/shard_map/all_gather | solution.py:99
  590.2 35.9 %while.31 = (s32[]{:T(128)}, f32[6,288]{1,0:T(8,128)S(1)}, f32[6,288]{1,0:T(8,128)S(1)}, f32[288,6,128]{2,0,1:T(8,128)S(1)}, bf16[2,1024,768]{2,1,0:T(8,128)(2,1...) while((s32[]{:T(128)}, f32[6,288]{1,0:T(8,128)S(1)}, ...), condition=%wide.region_13.14_spmd.clone, body=%wide.region_10.13_spmd.clone.sunk | while | flops 919029888 | bytes 67596424 | solution.py:43
  (175 shorter events, 182.5 us)
Async XLA Ops:
  7.2 475.1 %copy-start = (bf16[768,1536]{1,0:T(8,128)(2,1)S(1)}, bf16[768,1536]{1,0:T(8,128)(2,1)}, u32[]{:S(2)}) copy-start(bf16[768,1536]{1,0:T(8,128)(2,1)} %param.17) | copy-start | bytes 7077892
  7.2 3.5 copy-start.8
  7.2 153.3 %all-gather.4.cloned.1.call-start = ((), (), s32[]{:S(2)}) async-start(), calls=%async_computation.2 | async-start | bytes 14598144 | tf_op jit(solution)/shard_map/all_gather | solution.py:85
  30.1 4.0 copy-start.9
  30.1 257.2 %all-gather.6.cloned.1.call-start = ((), (), s32[]{:S(2)}) async-start(), calls=%async_computation.3 | async-start | bytes 14598144 | tf_op jit(solution)/shard_map/all_gather | solution.py:86
  32.5 463.8 %reduce-scatter.2.cloned.1.call-start = ((), (), s32[]{:S(2)}) async-start(), calls=%async_computation.4 | async-start | bytes 2654208 | tf_op jit(solution)/shard_map/reduce_scatter | solution.py:91
  301.8 5.5 copy-start.2
  323.4 5.5 copy-start.2
  345.1 5.5 copy-start.2
  366.7 5.5 copy-start.2
  388.4 5.5 copy-start.2
  410.0 5.5 copy-start.2
  431.7 5.5 copy-start.2
  453.4 5.5 copy-start.2
  475.0 5.5 copy-start.2
  482.2 2.2 copy-start.7
  486.4 9.8 %copy-start.5 = (bf16[144,1536]{1,0:T(8,128)(2,1)S(1)}, bf16[144,1536]{1,0:T(8,128)(2,1)}, u32[]{:S(2)}) copy-start(bf16[144,1536]{1,0:T(8,128)(2,1)} %param.14) | copy-start | bytes 1327108
  486.4 86.4 %all-to-all-start = ((bf16[32,64,768]{2,1,0:T(8,128)(2,1)}), bf16[32,64,768]{2,1,0:T(8,128)(2,1)}, u32[]{:S(2)}, u32[]{:S(2)}) async-start(bf16[32,64,768]{2,1,0:T(8,128)(2,1)} %stack.2), calls=%async_computation.1 | async-start | bytes 6291456 | tf_op jit(solution)/shard_map/all_to_all | solution.py:101
  492.3 97.9 %all-gather.8.cloned.1.call-start = ((), (), s32[]{:S(2)}) async-start(), calls=%async_computation.5 | async-start | bytes 3244032 | tf_op jit(solution)/shard_map/all_gather | solution.py:99
  496.2 4.1 copy-start.12
  497.7 2.6 copy-start.6
  601.4 5.1 copy-start.3
  619.3 5.1 copy-start.3
  626.1 1.8 copy-start.1
  (3 other events, 3.5 us)
Sparse Core Ops, SparseCore 0:
  30.3 130.1 all-gather.3
  163.0 124.2 all-gather.5
  484.5 11.6 reduce-scatter.1
  499.0 91.1 all-gather.7
